TPU v7x, 768 devices: a whole 4x8x12 slice. The times are simulated.
768 devices in a mesh: dp: 192 (over y, z_hi, x, core), expert: 4 (over z_lo).
Axes of the slice: x: 4, y: 8, z: 12 (z_hi: 3, z_lo: 4; z = z_hi * 4 + z_lo), core: 2. Of those that a mesh axis runs over, the one named last changes fastest.
Arguments:
- tokens: bfloat16 [49152, 6144], P(('dp', 'expert')), may hold values from -6 to 6
- expert_ids: int32 [49152, 2], P(('dp', 'expert')), may hold values from 0 to 7, all different within a row; in each aligned block of 64 rows (0 to 63, 64 to 127, ...) at most 18 rows name the same one
- gate_probs: float32 [49152, 2], P(('dp', 'expert')), may hold values from 0.2 to 1
- w_gate: bfloat16 [8, 64, 6144], P('expert'), may hold values from -0.078125 to 0.078125
- w_up: bfloat16 [8, 64, 6144], P('expert'), may hold values from -0.078125 to 0.078125
- w_down: bfloat16 [8, 64, 6144], P('expert'), may hold values from -0.75 to 0.75
- v_gate: bfloat16 [8, 64, 6144], P('expert'), may hold values from -0.078125 to 0.078125
- v_up: bfloat16 [8, 64, 6144], P('expert'), may hold values from -0.078125 to 0.078125
Outputs:
- curvature: float32 [6144, 1024], P('dp', 'expert')
Inputs may be any that keep to these rules, and one draw needn't show every extreme that they name: `expert_ids`: each token names two different experts; among the 64 tokens of one device (aligned blocks in order) at most 18 name any one expert, a bound that some block reaches.
All inputs are finite; a program needn't handle non-finite values.
Results may differ from a plain program's by a relative error of at most 0.02.
Values may be sent and summed in bfloat16 or wider, within the bound.
A program may use at most 64 MiB of HBM per device.

v0:
```python
import jax
import jax.numpy as jnp
from jax import lax
from jax.sharding import PartitionSpec as P


def local_terms(pre_act, width):
    gate_pre = pre_act[..., :width]
    up_pre = pre_act[..., width : 2 * width]
    gate_tan = pre_act[..., 2 * width : 3 * width]
    up_tan = pre_act[..., 3 * width :]
    sigmoid = jax.nn.sigmoid(gate_pre)
    silu_val = gate_pre * sigmoid
    slope = sigmoid * (1.0 + gate_pre * (1.0 - sigmoid))
    hidden_tan = slope * up_pre * gate_tan + silu_val * up_tan
    return (silu_val, slope * up_pre, hidden_tan)


def body(tokens, expert_ids, gate_probs, w_gate, w_up, w_down, v_gate, v_up):
    groups = lax.axis_size("expert")
    per_device = w_gate.shape[0]
    experts = groups * per_device
    token_count = tokens.shape[0]
    assigned = 2 * token_count
    model_width = tokens.shape[1]
    unit_count = w_gate.shape[1]
    capacity = token_count * 9 // 32
    total_tokens = token_count * lax.axis_size("dp") * groups
    flat_ids = expert_ids.reshape(assigned)
    flat_probs = gate_probs.reshape(assigned)
    expert_hot = (flat_ids[:, None] == jnp.arange(experts, dtype=jnp.int32)[None, :]).astype(
        jnp.float32
    )
    earlier = (
        lax.broadcasted_iota(jnp.int32, (assigned, assigned), 0)
        > lax.broadcasted_iota(jnp.int32, (assigned, assigned), 1)
    ).astype(jnp.float32)
    before = jnp.dot(earlier, expert_hot, precision=lax.Precision.HIGHEST)
    slot_pos = jnp.sum(before * expert_hot, axis=1)
    slot_hot = (slot_pos[:, None] == jnp.arange(capacity, dtype=jnp.float32)[None, :]).astype(
        jnp.float32
    )
    placing = (expert_hot[:, :, None] * slot_hot[:, None, :]).reshape(assigned, experts * capacity)
    placing_half = placing.astype(jnp.bfloat16)
    repeated = jnp.repeat(tokens, 2, axis=0)
    sent_rows = jnp.einsum(
        "as,ad->sd", placing_half, repeated, preferred_element_type=jnp.float32
    ).astype(jnp.bfloat16)
    sent_rows = sent_rows.reshape(groups, per_device, capacity, model_width)
    sent_probs = jnp.einsum(
        "as,a->s", placing, flat_probs, precision=lax.Precision.HIGHEST
    ).reshape(groups, per_device, capacity)
    arrived_rows, arrived_probs = (
        lax.all_to_all(sent_rows, "expert", split_axis=0, concat_axis=0, tiled=True),
        lax.all_to_all(
            sent_probs.astype(jnp.bfloat16), "expert", split_axis=0, concat_axis=0, tiled=True
        ).astype(sent_probs.dtype),
    )
    stacked = jnp.concatenate([w_gate, w_up, v_gate, v_up], axis=1)
    pre_act = jnp.einsum(
        "glcd,lfd->glcf", arrived_rows, stacked, preferred_element_type=jnp.float32
    )
    silu_val, slope_up, hidden_tan = local_terms(pre_act, unit_count)
    scaled = (arrived_probs[..., None] * hidden_tan).astype(jnp.bfloat16)
    term_rows = jnp.einsum(
        "glcf,lfd->glcd", scaled, w_down, preferred_element_type=jnp.float32
    ).astype(jnp.bfloat16)
    returned = lax.all_to_all(term_rows, "expert", split_axis=0, concat_axis=0, tiled=True)
    term_assign = jnp.einsum(
        "as,sd->ad",
        placing_half,
        returned.reshape(experts * capacity, model_width),
        preferred_element_type=jnp.float32,
    )
    adjoint = jnp.sum(term_assign.reshape(token_count, 2, model_width), axis=1).astype(jnp.bfloat16)
    adjoint_slots = jnp.einsum(
        "as,ad->sd",
        placing_half,
        jnp.repeat(adjoint, 2, axis=0),
        preferred_element_type=jnp.float32,
    ).astype(jnp.bfloat16)
    adjoint_slots = adjoint_slots.reshape(groups, per_device, capacity, model_width)
    arrived_adjoint = lax.all_to_all(
        adjoint_slots, "expert", split_axis=0, concat_axis=0, tiled=True
    )
    pulled = jnp.einsum(
        "glcd,lfd->glcf", arrived_adjoint, w_down, preferred_element_type=jnp.float32
    )
    weighted = arrived_probs[..., None] * pulled
    coef = jnp.concatenate(
        [(weighted * slope_up).astype(jnp.bfloat16), (weighted * silu_val).astype(jnp.bfloat16)],
        axis=-1,
    )
    own_rows = model_width // lax.axis_size("dp")
    block = jnp.einsum("glcd,glcj->dlj", arrived_rows, coef, preferred_element_type=jnp.float32)
    return lax.psum_scatter(
        block.reshape(own_rows * lax.axis_size("dp"), per_device * 2 * unit_count)
        * (1.0 / total_tokens),
        "dp",
        scatter_dimension=0,
        tiled=True,
    )


def solution(mesh):
    return jax.shard_map(
        body,
        mesh=mesh,
        in_specs=(
            P(("dp", "expert"), None),
            P(("dp", "expert"), None),
            P(("dp", "expert"), None),
            P("expert", None, None),
            P("expert", None, None),
            P("expert", None, None),
            P("expert", None, None),
            P("expert", None, None),
        ),
        out_specs=P("dp", "expert"),
        check_vma=False,
    )
```

profile of v0, /device:TPU:1, one launch (start us, length us, event | category | flops | bytes accessed | tf_op | source)
XLA Modules:
  0.0 1442.5 jit_solution(11867218028668412826)
XLA Ops:
  6.5 0.9 copy.40
  7.7 0.8 copy.43
  9.3 0.6 fusion.44
  9.9 0.6 convert_element_type.73
  10.5 7.8 all-to-all-start
  18.6 2.1 broadcast_in_dim.4
  20.6 1.5 reshape.100
  22.1 2.0 convolution_convert_fusion.2
  24.2 1.7 reshape.101
  25.9 4.7 copy.46
  30.6 4.5 all-to-all-start.1
  35.1 39.5 %all-to-all-done.1 = bf16[4,2,18,6144]{3,1,2,0:T(2,128)(2,1)S(1)} async-done(((bf16[4,2,18,6144]{3,1,2,0:T(2,128)(2,1)}), bf16[4,2,18,6144]{3,1,2,0:T(2,128)(2,1)S(1)}, u32[]{:S(2)}, u32[]{:S(2)}) %all-to-all-start.1) | async-done | bytes 1769504 | tf_op jit(solution)/shard_map/all_to_all | solution.py:54
  74.6 4.3 fusion.15
  78.9 0.8 fusion.1
  79.8 3.1 copy.48
  82.8 4.4 all-to-all-start.2
  87.2 0.2 reduce-scatter.2.cloned.1.call-start
  87.5 1.2 convert_element_type.77
  88.7 39.3 %all-to-all-done.2 = bf16[4,2,18,6144]{3,1,2,0:T(2,128)(2,1)} async-done(((bf16[4,2,18,6144]{3,1,2,0:T(2,128)(2,1)}), bf16[4,2,18,6144]{3,1,2,0:T(2,128)(2,1)}, u32[]{:S(2)}, u32[]{:S(2)}) %all-to-all-start.2) | async-done | bytes 1769504 | tf_op jit(solution)/shard_map/all_to_all | solution.py:68
  128.0 3.5 copy.49
  131.5 2.8 reshape.109
  134.3 2.1 convolution_reduce_fusion
  136.4 2.1 broadcast_in_dim.5
  138.5 4.5 reshape.103
  143.0 3.2 convolution_convert_fusion.1
  146.3 2.9 reshape.104
  149.1 3.5 copy.51
  152.6 43.1 %all_to_all.20 = bf16[4,2,18,6144]{3,1,2,0:T(2,128)(2,1)S(1)} all-to-all(bf16[4,2,18,6144]{3,1,2,0:T(2,128)(2,1)S(1)} %copy.51), channel_id=1, replica_groups=mesh['dp'=192,'expert'=4] {'expert'}, dimensions={0} | all-to-all | bytes 3538944 | tf_op jit(solution)/shard_map/all_to_all | solution.py:83
  195.7 1.1 multiply_convert_fusion.1
  196.8 4.6 fusion
  201.4 6.6 copy.54
  208.0 1227.7 %reduce-scatter.2.cloned.1.call-done = f32[32,256]{1,0:T(8,128)} async-done(((f32[6144,256]{1,0:T(8,128)}), f32[32,256]{1,0:T(8,128)}) %reduce-scatter.2.cloned.1.call-update) | async-done | bytes 32784 | tf_op jit(solution)/shard_map/reduce_scatter | solution.py:96
  (23 shorter events, 1.3 us)
Async XLA Ops:
  6.5 72.4 %copy-start = (bf16[2,64,6144]{2,1,0:T(8,128)(2,1)S(1)}, bf16[2,64,6144]{2,1,0:T(8,128)(2,1)}, u32[]{:S(2)}) copy-start(bf16[2,64,6144]{2,1,0:T(8,128)(2,1)} %param.13) | copy-start | bytes 4718596
  9.0 9.5 copy-start.1
  10.5 20.1 %all-to-all-start = ((bf16[4,2,18]{2,1,0:T(2,128)(2,1)}), bf16[4,2,18]{2,1,0:T(2,128)(2,1)S(1)}, u32[]{:S(2)}, u32[]{:S(2)}) async-start(bf16[4,2,18]{2,1,0:T(2,128)(2,1)} %convert_element_type.73), calls=%async_computation | async-start | bytes 4096 | tf_op jit(solution)/shard_map/all_to_all | solution.py:55
  30.6 44.0 %all-to-all-start.1 = ((bf16[4,2,18,6144]{3,1,2,0:T(2,128)(2,1)}), bf16[4,2,18,6144]{3,1,2,0:T(2,128)(2,1)S(1)}, u32[]{:S(2)}, u32[]{:S(2)}) async-start(bf16[4,2,18,6144]{3,1,2,0:T(2,128)(2,1)} %copy.46), calls=%async_computation.1 | async-start | bytes 3538944 | tf_op jit(solution)/shard_map/all_to_all | solution.py:54
  78.9 0.8 copy-start.2
  82.8 45.1 %all-to-all-start.2 = ((bf16[4,2,18,6144]{3,1,2,0:T(2,128)(2,1)}), bf16[4,2,18,6144]{3,1,2,0:T(2,128)(2,1)}, u32[]{:S(2)}, u32[]{:S(2)}) async-start(bf16[4,2,18,6144]{3,1,2,0:T(2,128)(2,1)} %copy.48), calls=%async_computation.2 | async-start | bytes 3538944 | tf_op jit(solution)/shard_map/all_to_all | solution.py:68
  87.2 1348.4 %reduce-scatter.2.cloned.1.call-start = ((), (), s32[]{:S(2)}) async-start(), calls=%async_computation.5 | async-start | bytes 6324224 | tf_op jit(solution)/shard_map/reduce_scatter | solution.py:96
  152.6 43.1 %copy-start.3 = (f32[4,2,18,256]{3,2,0,1:T(8,128)S(1)}, f32[4,2,18,256]{3,2,0,1:T(8,128)}, u32[]{:S(2)}) copy-start(f32[4,2,18,256]{3,2,0,1:T(8,128)} %copy-done.2) | copy-start | bytes 442372
Sparse Core Ops, SparseCore 0:
  208.1 1227.4 reduce-scatter.1
where the time goes:
time: 1450 us; the launch traced here: 1440 us
  waiting for transfers between devices  1310 us (90%)
  blocking collectives  43.1 us (3%)
  local copies, waits for them, and re-layouts  42.7 us (3%)
  matrix products  18.9 us (1%)
  starting transfers between devices  17 us (1%)
    reduce_scatter x1, waiting for transfers between devices, body(): lax.psum_scatter(block.reshape(own_rows * lax.axis_size('dp'), per_device...  1230 us
    all_to_all x1, blocking collectives, body(): lax.all_to_all(adjoint_slots, 'expert', split_axis=0, concat_axis=0, tile...  43.1 us
    all_to_all x1, waiting for transfers between devices, body(): lax.all_to_all(sent_rows, 'expert', split_axis=0, concat_axis=0, tiled=True)  39.5 us
    all_to_all x1, waiting for transfers between devices, body(): lax.all_to_all(term_rows, 'expert', split_axis=0, concat_axis=0, tiled=True)  39.3 us
  transfers between devices with their start and end apart: 4, of which 3 were waited for; matrix products, arithmetic and copies ran while one was open for 1% of the time, Pallas kernels for 0%

commit v1 on v0

v1 whole, which is shorter than its diff:
```python
import functools

import jax
import jax.numpy as jnp
from jax import lax
from jax.experimental import pallas as pl
from jax.experimental.pallas import tpu as pltpu
from jax.sharding import PartitionSpec as P

F32 = jnp.float32
BF16 = jnp.bfloat16
GRID = (8, 3, 4, 2)


def iota(shape, dim):
    return lax.broadcasted_iota(jnp.int32, shape, dim)


def dot(a, b, dims=((1,), (0,)), precision=None):
    return lax.dot_general(a, b, (dims, ((), ())), precision=precision, preferred_element_type=F32)


def one_hot(mask):
    return jnp.where(mask, 1.0, 0.0).astype(BF16)


def kernel(
    cfg,
    meta_ref, tokens_ref, part_ref, wg_ref, wu_ref, vg_ref, vu_ref, wd_ref,
    out_ref,
    meta_all, parts, weights, down, sent, sent_tail, rows, tails, pre, g_all, g_own,
    scaled_all, partial, core_send, core_recv, z_acc, z_send, z_recv,
    ax_s, ax_r, ay_s, ay_r, bx_s, bx_r, by_s, by_r,
    w_sem, meta_sem, part_sem, row_sem, tail_sem, sc_sem, core_sem, g_sem, rs_sem, z_sem,
):
    ny, nz, nx, nc, ne, cap = cfg
    width = tokens_ref.shape[1]
    slots = 2 * cap
    main = slots // 16 * 16
    rest = slots - main
    chunks = 16 // rest
    cw = width // chunks
    n_rows = ne * slots
    n_main = ne * main
    plane = ny * nx * nc
    r2 = 128 // plane
    g_parts = 16 // r2
    pw = width // g_parts

    dp = lax.axis_index("dp")
    e = lax.axis_index("expert")
    c = lax.rem(dp, nc)
    x = lax.rem(dp // nc, nx)
    zh = lax.rem(dp // (nc * nx), nz)
    y = dp // (nc * nx * nz)

    def at(yy=y, zz=zh, xx=x, cc=c):
        return ((yy * nz + zz) * nx + xx) * nc + cc

    def turn(v, k, n):
        return lax.rem(v + k + n, n)

    def remote(src, dst, s_sem, r_sem, dev):
        copy = pltpu.make_async_remote_copy(
            src_ref=src, dst_ref=dst, send_sem=s_sem, recv_sem=r_sem,
            device_id=dev, device_id_type=pl.DeviceIdType.MESH,
        )
        copy.start()
        return copy

    pending = []

    w_copies = []
    for m, ref in enumerate((wg_ref, wu_ref, vg_ref, vu_ref)):
        cp = pltpu.make_async_copy(ref, weights.at[pl.ds(m * 128, 128)], w_sem.at[m])
        cp.start()
        w_copies.append(cp)
    down_copy = pltpu.make_async_copy(wd_ref, down, w_sem.at[4])
    down_copy.start()

    peers = [(dp, turn(e, k, ne)) for k in range(1, ne)]
    for k in sorted({1, ny - 1} - {0}):
        peers.append((at(yy=turn(y, k, ny)), e))
    for k in sorted({1, nx - 1} - {0}):
        peers.append((at(xx=turn(x, k, nx)), e))
    for k in range(1, nz):
        peers.append((at(zz=turn(zh, k, nz)), e))
    for k in range(1, nc):
        peers.append((at(cc=turn(c, k, nc)), e))
    barrier = pltpu.get_barrier_semaphore()
    for dev in peers:
        pl.semaphore_signal(barrier, inc=1, device_id=dev, device_id_type=pl.DeviceIdType.MESH)
    pl.semaphore_wait(barrier, len(peers))

    meta_copies, part_copies = [], []
    for k in range(1, ne):
        dev = (dp, turn(e, k, ne))
        meta_copies.append(remote(meta_ref, meta_all.at[e], meta_sem.at[0, k - 1], meta_sem.at[1, k - 1], dev))
    for k in range(1, ne):
        dev = (dp, turn(e, k, ne))
        part_copies.append(remote(part_ref, parts.at[e], part_sem.at[0, k - 1], part_sem.at[1, k - 1], dev))
    meta_all[e] = meta_ref[...]
    parts[e] = part_ref[...]

    lanes = 128
    upper = one_hot(iota((lanes, lanes), 0) < iota((lanes, lanes), 1))

    def slot_of(meta):
        ids = meta[0:1, :].astype(jnp.int32)
        hot = iota((2 * ne, lanes), 0) == ids
        before = dot(one_hot(hot), upper)
        where = before + cap * iota((2 * ne, lanes), 0).astype(F32)
        return jnp.sum(jnp.where(hot, where, 0.0), axis=0, keepdims=True).astype(jnp.int32)

    g_mine = slot_of(meta_ref[...])
    half = one_hot((iota((lanes, lanes // 2), 0) >> 1) == iota((lanes, lanes // 2), 1))
    r_main = iota((n_main, lanes), 0)
    slot_main = (r_main // main) * slots + r_main % main
    pick_main = dot(one_hot(slot_main == g_mine), half).astype(BF16)
    n_tail = ne * 16
    r_tail = iota((n_tail, lanes), 0)
    slot_tail = (r_tail // 16) * slots + main + r_tail % rest
    q_tail = (r_tail % 16) // rest
    hit_tail = slot_tail == g_mine
    tail_val = jnp.zeros((n_tail, cw), F32)
    for q in range(chunks):
        pick = dot(one_hot(hit_tail & (q_tail == q)), half).astype(BF16)
        tail_val = tail_val + dot(pick, tokens_ref[:, q * cw : (q + 1) * cw])
    tail_val = tail_val.astype(BF16)
    for d in range(ne):
        sent_tail[d] = tail_val[d * 16 : (d + 1) * 16]
    tail_copies = []
    row_copies = []
    for q in range(chunks):
        cols = slice(q * cw, (q + 1) * cw)
        val = dot(pick_main, tokens_ref[:, cols]).astype(BF16)
        for d in range(ne):
            sent[d, :, cols] = val[d * main : (d + 1) * main]
        got = []
        for k in (2, 1, 3) if ne == 4 else range(1, ne):
            d = turn(e, k, ne)
            got.append(
                remote(
                    sent.at[d, :, pl.ds(q * cw, cw)],
                    rows.at[pl.ds(pl.multiple_of(e * main, 16), main), pl.ds(q * cw, cw)],
                    row_sem.at[0, q, k - 1], row_sem.at[1, q, k - 1], (dp, d),
                )
            )
            if q == 0:
                tail_copies.append(
                    remote(sent_tail.at[d], tails.at[e], tail_sem.at[0, k - 1], tail_sem.at[1, k - 1], (dp, d))
                )
        row_copies.append(got)
        rows[pl.ds(pl.multiple_of(e * main, 16), main), cols] = sent[e, :, cols]
    tails[e] = sent_tail[e]

    down_copy.wait()
    for cp in part_copies:
        cp.wait()
    gw = parts[...].reshape(ne * 16, pw)
    acc = jnp.zeros((ne * 16, 128), F32)
    r_part = iota((ne * 16, 128), 0) % 16 // r2
    for i in range(g_parts):
        acc = acc + jnp.where(r_part == i, dot(gw, down[:, i * pw : (i + 1) * pw], ((1,), (1,))), 0.0)
    g_rows = ne * r2
    to_row = iota((g_rows, ne * 16), 0)
    from_row = iota((g_rows, ne * 16), 1)
    collect = jnp.where((from_row // 16 == to_row // r2) & (from_row % r2 == to_row % r2), 1.0, 0.0)
    g_all[y, x, c] = dot(collect, acc, precision=lax.Precision.HIGHEST)

    def gather(block, me, n, dev, base):
        right = n // 2
        left = n - 1 - right
        r_cp, l_cp = [], []
        if right:
            r_cp.append(remote(block(me), block(me), g_sem.at[0, base], g_sem.at[1, base], dev(1)))
        if left:
            l_cp.append(remote(block(me), block(me), g_sem.at[0, base + 4], g_sem.at[1, base + 4], dev(-1)))
        for k in range(right):
            r_cp[k].wait_recv()
            if k + 1 < right:
                b = block(turn(me, -1 - k, n))
                s = base + k + 1
                r_cp.append(remote(b, b, g_sem.at[0, s], g_sem.at[1, s], dev(1)))
            if k < left:
                l_cp[k].wait_recv()
                if k + 1 < left:
                    b = block(turn(me, 1 + k, n))
                    s = base + 4 + k + 1
                    l_cp.append(remote(b, b, g_sem.at[0, s], g_sem.at[1, s], dev(-1)))
        pending.extend(r_cp + l_cp)

    gather(lambda i: g_all.at[y, x, i], c, nc, lambda k: (at(cc=turn(c, k, nc)), e), 0)
    gather(lambda i: g_all.at[y, i], x, nx, lambda k: (at(xx=turn(x, k, nx)), e), 8)
    gather(lambda i: g_all.at[i], y, ny, lambda k: (at(yy=turn(y, k, ny)), e), 16)

    for cp in meta_copies:
        cp.wait()
    r_all = iota((n_rows, lanes), 0)
    in_main = r_all < n_main
    src_all = jnp.where(in_main, r_all // main, (r_all - n_main) // rest)
    slot_all = jnp.where(in_main, r_all % main, main + (r_all - n_main) % rest)
    same = one_hot((iota((lanes, lanes), 0) >> 1) == (iota((lanes, lanes), 1) >> 1))
    g_src = [slot_of(meta_all[s]) for s in range(ne)]
    prob = jnp.zeros((n_rows, 1), F32)
    mine = []
    for s in range(ne):
        hit = (src_all == s) & (slot_all + e * slots == g_src[s])
        prob = prob + jnp.sum(jnp.where(hit, meta_all[s][1:2, :], 0.0), axis=1, keepdims=True)
        mine.append(dot(one_hot(hit), same).astype(BF16))
    links = []
    for q in range(ne):
        total = jnp.zeros((n_rows, n_rows), F32)
        for s in range(ne):
            hit = one_hot((src_all == s) & (slot_all + q * slots == g_src[s]))
            total = total + dot(mine[s], hit, ((1,), (1,)))
        links.append(total.astype(BF16))
    flat_g = g_all[...].reshape(plane * g_rows, 128).astype(BF16)
    p_row = iota((128, plane * g_rows), 0)
    p_col = iota((128, plane * g_rows), 1)
    for q in range(ne):
        perm = one_hot(p_col == (p_row // r2) * g_rows + q * r2 + p_row % r2)
        g_own[q] = dot(perm, flat_g).astype(BF16)

    for cp in w_copies:
        cp.wait()
    for cp in tail_copies:
        cp.wait()
    t_row = iota((ne * rest, n_tail), 0)
    t_col = iota((ne * rest, n_tail), 1)
    flat_tails = tails[...].reshape(n_tail, cw)
    for q in range(chunks):
        hit = (t_row // rest == t_col // 16) & (t_col % 16 == q * rest + t_row % rest)
        rows[n_main:n_rows, q * cw : (q + 1) * cw] = dot(one_hot(hit), flat_tails).astype(BF16)
    for q in range(chunks):
        for cp in row_copies[q]:
            cp.wait()
        cols = slice(q * cw, (q + 1) * cw)
        val = dot(rows[:, cols], weights[:, cols], ((1,), (1,)))
        if q == 0:
            pre[...] = val
        else:
            pre[...] += val

    gate_pre, up_pre = pre[:, 0:128], pre[:, 128:256]
    gate_tan, up_tan = pre[:, 256:384], pre[:, 384:512]
    sigmoid = jax.nn.sigmoid(gate_pre)
    silu_val = gate_pre * sigmoid
    slope_up = sigmoid * (1.0 + gate_pre * (1.0 - sigmoid)) * up_pre
    hidden_tan = slope_up * gate_tan + silu_val * up_tan
    valid = (iota((n_rows, 128), 1) // 64) == jnp.where(slot_all >= cap, 1, 0)
    scaled_all[e] = jnp.where(valid, prob * hidden_tan, 0.0).astype(BF16)
    sc_copies = [
        remote(scaled_all.at[e], scaled_all.at[e], sc_sem.at[0, k - 1], sc_sem.at[1, k - 1], (dp, turn(e, k, ne)))
        for k in range(1, ne)
    ]
    for cp in sc_copies:
        cp.wait()
    pulled = jnp.zeros((n_rows, 128), F32)
    for q in range(ne):
        pulled = pulled + dot(dot(links[q], scaled_all[q]).astype(BF16), g_own[q])
    weighted = jnp.where(valid, prob * pulled, 0.0)
    coef_gate = weighted * slope_up
    coef_up = weighted * silu_val
    low = iota((n_rows, 128), 1) < 64
    coef = jnp.concatenate(
        [
            jnp.where(low, coef_gate, pltpu.roll(coef_up, 64, 1)),
            jnp.where(low, pltpu.roll(coef_gate, 64, 1), coef_up),
        ],
        axis=1,
    ).astype(BF16)

    span = width // ny
    own = width // (ny * nz * nx * nc)
    core_copies = []
    for i in range(ny):
        part = dot(rows[:, i * span : (i + 1) * span], coef, ((0,), (0,)))
        partial[i] = part.reshape(nz, nx, nc, own, 256)
        if nc == 2:
            core_send[i] = partial[i, :, :, 1 - c].astype(BF16)
            core_copies.append(
                remote(core_send.at[i], core_recv.at[i], core_sem.at[0, i], core_sem.at[1, i], (at(cc=1 - c), e))
            )
    for cp in core_copies:
        cp.wait()
    for i in range(ny if nc == 2 else 0):
        partial[i, :, :, c] += core_recv[i].astype(F32)

    def ring(own_block, me, n, dev, s_buf, r_buf, base, long_right):
        right = n // 2 if long_right else n - 1 - n // 2
        left = n - 1 - right
        r_cp, l_cp = [], []
        for k in range(max(right, left)):
            if k < right:
                val = own_block(turn(me, right - k, n))
                if k:
                    r_cp[k - 1].wait_recv()
                    val = val + r_buf[k - 1].astype(F32)
                s_buf[k] = val.astype(BF16)
                r_cp.append(remote(s_buf.at[k], r_buf.at[k], rs_sem.at[0, base + k], rs_sem.at[1, base + k], dev(1)))
            if k < left:
                j = right + k
                val = own_block(turn(me, k - left, n))
                if k:
                    l_cp[k - 1].wait_recv()
                    val = val + r_buf[j - 1].astype(F32)
                s_buf[j] = val.astype(BF16)
                l_cp.append(remote(s_buf.at[j], r_buf.at[j], rs_sem.at[0, base + j], rs_sem.at[1, base + j], dev(-1)))
            yield None
        total = own_block(me)
        if right:
            r_cp[-1].wait_recv()
            total = total + r_buf[right - 1].astype(F32)
        if left:
            l_cp[-1].wait_recv()
            total = total + r_buf[right + left - 1].astype(F32)
        pending.extend(r_cp + l_cp)
        yield total

    dev_x = lambda k: (at(xx=turn(x, k, nx)), e)
    dev_y = lambda k: (at(yy=turn(y, k, ny)), e)

    def path_a():
        for total in ring(lambda t: partial[:, :, t, c, :, 0:128], x, nx, dev_x, ax_s, ax_r, 0, True):
            if total is None:
                yield
        partial[:, :, x, c, :, 0:128] = total
        for total in ring(lambda t: partial[t, :, x, c, :, 0:128], y, ny, dev_y, ay_s, ay_r, 4, False):
            if total is None:
                yield
        z_acc[:, :, 0:128] = total

    def path_b():
        for total in ring(lambda t: partial[t, :, :, c, :, 128:256], y, ny, dev_y, by_s, by_r, 12, True):
            if total is None:
                yield
        partial[y, :, :, c, :, 128:256] = total
        for total in ring(lambda t: partial[y, :, t, c, :, 128:256], x, nx, dev_x, bx_s, bx_r, 20, False):
            if total is None:
                yield
        z_acc[:, :, 128:256] = total

    live = [path_b(), path_a()]
    while live:
        for path in list(live):
            try:
                next(path)
            except StopIteration:
                live.remove(path)

    result = z_acc[zh]
    z_copies = []
    for k in range(1, nz):
        t = turn(zh, k, nz)
        z_send[k - 1] = z_acc[t].astype(BF16)
        z_copies.append(
            remote(z_send.at[k - 1], z_recv.at[k - 1], z_sem.at[0, k - 1], z_sem.at[1, k - 1], (at(zz=t), e))
        )
    for k, cp in enumerate(z_copies):
        cp.wait()
        result = result + z_recv[k].astype(F32)
    out_ref[...] = result
    for cp in pending:
        cp.wait_send()


def fused(cfg, meta, tokens, part, mats):
    ny, nz, nx, nc, ne, cap = cfg
    width = tokens.shape[1]
    slots = 2 * cap
    main = slots // 16 * 16
    rest = slots - main
    chunks = 16 // rest
    n_rows = ne * slots
    plane = ny * nx * nc
    r2 = 128 // plane
    own = width // (ny * nz * nx * nc)
    vmem, dma = pltpu.VMEM, pltpu.SemaphoreType.DMA
    vspec = pl.BlockSpec(memory_space=pltpu.VMEM)
    hspec = pl.BlockSpec(memory_space=pl.ANY)
    hx, hy = max(nx - 1, 1), max(ny - 1, 1)
    return pl.pallas_call(
        functools.partial(kernel, cfg),
        out_shape=jax.ShapeDtypeStruct((own, 256), F32),
        in_specs=[vspec] * 3 + [hspec] * 5,
        out_specs=vspec,
        scratch_shapes=[
            vmem((ne, 8, 128), F32),
            vmem((ne,) + part.shape, BF16),
            vmem((512, width), BF16),
            vmem((128, width), BF16),
            vmem((ne, main, width), BF16),
            vmem((ne, 16, width // chunks), BF16),
            vmem((n_rows, width), BF16),
            vmem((ne, 16, width // chunks), BF16),
            vmem((n_rows, 512), F32),
            vmem((ny, nx, nc, ne * r2, 128), F32),
            vmem((ne, 128, 128), BF16),
            vmem((ne, n_rows, 128), BF16),
            vmem((ny, nz, nx, nc, own, 256), F32),
            vmem((ny, nz, nx, own, 256), BF16),
            vmem((ny, nz, nx, own, 256), BF16),
            vmem((nz, own, 256), F32),
            vmem((max(nz - 1, 1), own, 256), BF16),
            vmem((max(nz - 1, 1), own, 256), BF16),
            vmem((hx, ny, nz, own, 128), BF16),
            vmem((hx, ny, nz, own, 128), BF16),
            vmem((hy, nz, own, 128), BF16),
            vmem((hy, nz, own, 128), BF16),
            vmem((hx, nz, own, 128), BF16),
            vmem((hx, nz, own, 128), BF16),
            vmem((hy, nz, nx, own, 128), BF16),
            vmem((hy, nz, nx, own, 128), BF16),
            dma((5,)),
            dma((2, ne - 1)),
            dma((2, ne - 1)),
            dma((2, chunks, ne - 1)),
            dma((2, ne - 1)),
            dma((2, ne - 1)),
            dma((2, ny)),
            dma((2, 24)),
            dma((2, 24)),
            dma((2, max(nz - 1, 1))),
        ],
        compiler_params=pltpu.CompilerParams(
            collective_id=0, has_side_effects=True, vmem_limit_bytes=58 * 2**20
        ),
    )(meta, tokens, part, *mats)


def body(cfg, tokens, expert_ids, gate_probs, w_gate, w_up, w_down, v_gate, v_up):
    ny, nz, nx, nc, ne, cap = cfg
    width = tokens.shape[1]
    total_tokens = tokens.shape[0] * ny * nz * nx * nc * ne
    meta = jnp.stack([expert_ids.reshape(-1).astype(F32), gate_probs.reshape(-1)])
    meta = jnp.pad(meta, ((0, 6), (0, 0)))
    mats = [w.reshape(128, width) for w in (w_gate, w_up, v_gate, v_up, w_down)]
    dp = lax.axis_index("dp")
    place = (dp // (nc * nx * nz)) * (nx * nc) + dp % (nx * nc)
    r2 = 128 // (ny * nx * nc)
    part = lax.dynamic_slice(mats[4], (place * r2, 0), (r2, width))
    part = part.reshape(r2, 16 // r2, width * r2 // 16).transpose(1, 0, 2).reshape(16, -1)
    return fused(cfg, meta, tokens, part, mats) * (1.0 / total_tokens)


def solution(mesh, grid=GRID):
    cfg = grid + (mesh.shape["expert"], 18)
    return jax.shard_map(
        functools.partial(body, cfg),
        mesh=mesh,
        in_specs=(
            P(("dp", "expert"), None),
            P(("dp", "expert"), None),
            P(("dp", "expert"), None),
            P("expert", None, None),
            P("expert", None, None),
            P("expert", None, None),
            P("expert", None, None),
            P("expert", None, None),
        ),
        out_specs=P("dp", "expert"),
        check_vma=False,
    )
```

time: 1450 us -> 108 us (0.07)
  the two profiles are of different devices: /device:TPU:1 before, /device:TPU:2 now
where the time goes in v1:
time: 108 us
  Pallas kernels  102 us (94%)
  local copies, waits for them, and re-layouts  2.68 us (2%)
  other arithmetic  2.66 us (2%)
    pallas_call x1, Pallas kernels, fused(): pl.pallas_call(functools.partial(kernel, cfg), out_shape=jax.ShapeDtypeSt...  102 us

profile of v1, /device:TPU:2, one launch (start us, length us, event | category | flops | bytes accessed | tf_op | source)
XLA Modules:
  0.0 107.7 jit_solution(13496530082872788450)
XLA Ops:
  0.0 0.7 convert_element_type.15
  0.7 0.9 constant_dynamic-slice_fusion
  1.6 0.6 reshape.35.part_ref
  2.2 0.1 copy.11
  2.3 0.1 convert_element_type.16
  2.5 0.8 copy.12
  3.2 0.1 stack_reshape.3
  3.4 0.6 select_maximum_fusion.meta_ref
  4.0 102.3 %shard_map.82 = f32[32,256]{1,0:T(8,128)} custom-call(f32[8,128]{1,0:T(8,128)} %select_maximum_fusion.meta_ref, bf16[64,6144]{1,0:T(8,128)(2,1)} %tokens_ref.1, bf16[16,768]{1,0:T(8,128)(2,1)} %reshape.35.part_ref, bf16[128,6144]{1,0:T(8,128)(2,1)} %bitcast.10, bf16[128,6144]{1,0:T(8,128)(2,1)} %bitcast.11, bf16[128,6144]{1,0:T(8,128)(2,1)} %bitcast.12, ...), custom_call_target="tpu_custom_call" | custom-call | tf_op jit(solution)/shard_map/pallas_call | solution.py:383
  106.3 1.4 %broadcast_multiply_fusion = f32[32,256]{1,0:T(8,128)} fusion(f32[32,256]{1,0:T(8,128)} %shard_map.82), kind=kLoop, calls=%fused_computation | loop fusion | flops 8192 | bytes 65536 | tf_op jit(solution)/shard_map/mul | solution.py:444

commit v2 on v1

v2 whole, which is shorter than its diff:
```python
import functools

import jax
import jax.numpy as jnp
from jax import lax
from jax.experimental import pallas as pl
from jax.experimental.pallas import tpu as pltpu
from jax.sharding import PartitionSpec as P

F32 = jnp.float32
BF16 = jnp.bfloat16
GRID = (8, 3, 4, 2)


def iota(shape, dim):
    return lax.broadcasted_iota(jnp.int32, shape, dim)


def dot(a, b, dims=((1,), (0,)), precision=None):
    return lax.dot_general(a, b, (dims, ((), ())), precision=precision, preferred_element_type=F32)


def one_hot(mask):
    return jnp.where(mask, 1.0, 0.0).astype(BF16)


def kernel(
    cfg,
    ids_ref, probs_ref, tokens_ref, wg_ref, wu_ref, vg_ref, vu_ref, wd_ref,
    out_ref,
    meta_own, meta_all, part_own, parts, raw, weights, down, ordered, sent, sent_tail, rows, tails, pre,
    g_all, g_own, scaled_all, gathered, coef_all, coefs, partial, core_send, core_recv,
    z_acc, z_send, z_recv, ring_s, ring_r,
    w_sem, meta_sem, part_sem, row_sem, tail_sem, x_sem, sc_sem, coef_sem, core_sem, g_sem, rs_sem, z_sem,
):
    ny, nz, nx, nc, ne, cap = cfg
    width = tokens_ref.shape[1]
    slots = 2 * cap
    main = slots // 16 * 16
    rest = slots - main
    tail_parts = 16 // rest
    tw = width // tail_parts
    cw = width // nx
    n_rows = ne * slots
    n_main = ne * main
    n_tail = ne * 16
    plane = ny * nx * nc
    r2 = 128 // plane
    g_parts = 16 // r2
    pw = width // g_parts
    own = width // (ny * nz * nx * nc)

    dp = lax.axis_index("dp")
    e = lax.axis_index("expert")
    c = lax.rem(dp, nc)
    x = lax.rem(dp // nc, nx)
    zh = lax.rem(dp // (nc * nx), nz)
    y = dp // (nc * nx * nz)

    def at(yy=y, zz=zh, xx=x, cc=c):
        return ((yy * nz + zz) * nx + xx) * nc + cc

    def turn(v, k, n):
        return lax.rem(v + k + n, n)

    def remote(src, dst, s_sem, r_sem, dev):
        copy = pltpu.make_async_remote_copy(
            src_ref=src, dst_ref=dst, send_sem=s_sem, recv_sem=r_sem,
            device_id=dev, device_id_type=pl.DeviceIdType.MESH,
        )
        copy.start()
        return copy

    w_copies = []
    for m, ref in enumerate((wg_ref, wu_ref, vg_ref, vu_ref)):
        cp = pltpu.make_async_copy(ref, raw.at[pl.ds(m * 128, 128)], w_sem.at[m])
        cp.start()
        w_copies.append(cp)
    down_copy = pltpu.make_async_copy(wd_ref, down, w_sem.at[4])
    down_copy.start()

    peers = [(dp, turn(e, k, ne)) for k in range(1, ne)]
    for k in range(1, ny):
        peers.append((at(yy=turn(y, k, ny)), e))
    for k in range(1, nx):
        peers.append((at(xx=turn(x, k, nx)), e))
    for k in range(1, nz):
        peers.append((at(zz=turn(zh, k, nz)), e))
    for k in range(1, nc):
        peers.append((at(cc=turn(c, k, nc)), e))
    barrier = pltpu.get_barrier_semaphore()
    for dev in peers:
        pl.semaphore_signal(barrier, inc=1, device_id=dev, device_id_type=pl.DeviceIdType.MESH)

    lanes = 128
    upper = one_hot(iota((lanes, lanes), 0) < iota((lanes, lanes), 1))

    def slot_of(meta):
        ids = meta[0:1, :].astype(jnp.int32)
        hot = iota((2 * ne, lanes), 0) == ids
        before = dot(one_hot(hot), upper)
        where = before + cap * iota((2 * ne, lanes), 0).astype(F32)
        return jnp.sum(jnp.where(hot, where, 0.0), axis=0, keepdims=True).astype(jnp.int32)

    ids = ids_ref[...].astype(F32)
    probs = probs_ref[...]
    meta = jnp.concatenate(
        [
            jnp.concatenate([ids[0:1, :], ids[1:2, :]], axis=1),
            jnp.concatenate([probs[0:1, :], probs[1:2, :]], axis=1),
            jnp.zeros((6, lanes), F32),
        ],
        axis=0,
    )
    meta_own[...] = meta
    meta_all[e] = meta
    g_mine = slot_of(meta)
    half = one_hot(iota((lanes, lanes // 2), 0) % 64 == iota((lanes, lanes // 2), 1))
    r_main = iota((n_main, lanes), 0)
    slot_main = (r_main // main) * slots + r_main % main
    pick_main = dot(one_hot(slot_main == g_mine), half).astype(BF16)
    r_tail = iota((n_tail, lanes), 0)
    slot_tail = (r_tail // 16) * slots + main + r_tail % rest
    q_tail = (r_tail % 16) // rest
    hit_tail = slot_tail == g_mine

    def reorder(src, dst, rows_of):
        low = iota((rows_of, 128), 1) < 64

        def pair(m, carry):
            for h in range(nx // 2):
                first = src[:, pl.ds(pl.multiple_of((2 * m * (nx // 2) + h) * 128, 128), 128)]
                second = src[:, pl.ds(pl.multiple_of(((2 * m + 1) * (nx // 2) + h) * 128, 128), 128)]
                dst[:, pl.ds(pl.multiple_of(2 * h * cw + m * 128, 128), 128)] = jnp.where(
                    low, first, pltpu.roll(second, 64, 1)
                )
                dst[:, pl.ds(pl.multiple_of((2 * h + 1) * cw + m * 128, 128), 128)] = jnp.where(
                    low, pltpu.roll(first, 64, 1), second
                )
            return carry

        lax.fori_loop(0, ny * nz // 2, pair, 0)

    reorder(tokens_ref, ordered, tokens_ref.shape[0])

    order = [2, 1, 3, 0] if nx == 4 else list(range(1, nx)) + [0]
    z_order = (2, 1, 3) if ne == 4 else tuple(range(1, ne))

    def columns(k):
        return pl.ds(pl.multiple_of(turn(x, k, nx) * cw, 128), cw)

    def place_rows(k):
        val = dot(pick_main, ordered[:, columns(k)]).astype(BF16)
        for d in range(ne):
            sent[d, :, columns(k)] = val[d * main : (d + 1) * main]

    my_rows = pl.ds(pl.multiple_of(e * main, 16), main)

    def send_rows(k):
        got = []
        for j in z_order:
            d = turn(e, j, ne)
            got.append(
                remote(
                    sent.at[d, :, columns(k)], rows.at[my_rows, columns(k)],
                    row_sem.at[0, k, j - 1], row_sem.at[1, k, j - 1], (dp, d),
                )
            )
        rows[my_rows, columns(k)] = sent[e, :, columns(k)]
        return got

    place_rows(order[0])
    pl.semaphore_wait(barrier, len(peers))

    meta_copies, tail_copies, part_copies, row_copies = [], [], [], {}
    for j in range(1, ne):
        meta_copies.append(
            remote(meta_own, meta_all.at[e], meta_sem.at[0, j - 1], meta_sem.at[1, j - 1], (dp, turn(e, j, ne)))
        )
    row_copies[order[0]] = send_rows(order[0])
    tail_val = jnp.zeros((n_tail, tw), F32)
    for q in range(tail_parts):
        pick = dot(one_hot(hit_tail & (q_tail == q)), half).astype(BF16)
        tail_val = tail_val + dot(pick, ordered[:, q * tw : (q + 1) * tw])
    tail_val = tail_val.astype(BF16)
    for d in range(ne):
        sent_tail[d] = tail_val[d * 16 : (d + 1) * 16]
    for j in z_order:
        d = turn(e, j, ne)
        tail_copies.append(
            remote(sent_tail.at[d], tails.at[e], tail_sem.at[0, j - 1], tail_sem.at[1, j - 1], (dp, d))
        )
    tails[e] = sent_tail[e]
    down_copy.wait()
    s_row = iota((16, 128), 0)
    s_col = iota((16, 128), 1)
    first = ((y * nx + x) * nc + c) * r2
    for i in range(g_parts):
        pick = one_hot((s_row // r2 == i) & (s_col == first + s_row % r2))
        val = dot(pick, down[:, i * pw : (i + 1) * pw])
        part_val = val if i == 0 else part_val + val
    part_own[...] = part_val.astype(BF16)
    parts[e] = part_own[...]
    for j in z_order:
        part_copies.append(
            remote(part_own, parts.at[e], part_sem.at[0, j - 1], part_sem.at[1, j - 1], (dp, turn(e, j, ne)))
        )
    for k in order[1:]:
        place_rows(k)
        row_copies[k] = send_rows(k)

    for cp in tail_copies:
        cp.wait()
    t_row = iota((ne * rest, n_tail), 0)
    t_col = iota((ne * rest, n_tail), 1)
    flat_tails = tails[...].reshape(n_tail, tw)
    for q in range(tail_parts):
        hit = (t_row // rest == t_col // 16) & (t_col % 16 == q * rest + t_row % rest)
        rows[n_main:n_rows, q * tw : (q + 1) * tw] = dot(one_hot(hit), flat_tails).astype(BF16)

    for cp in part_copies:
        cp.wait()
    gw = parts[...].reshape(ne * 16, pw)
    acc = jnp.zeros((ne * 16, 128), F32)
    r_part = iota((ne * 16, 128), 0) % 16 // r2
    for i in range(g_parts):
        acc = acc + jnp.where(r_part == i, dot(gw, down[:, i * pw : (i + 1) * pw], ((1,), (1,))), 0.0)
    g_rows = ne * r2
    to_row = iota((g_rows, ne * 16), 0)
    from_row = iota((g_rows, ne * 16), 1)
    collect = jnp.where((from_row // 16 == to_row // r2) & (from_row % r2 == to_row % r2), 1.0, 0.0)
    g_all[y, x, c] = dot(collect, acc, precision=lax.Precision.HIGHEST)

    def share(block, n, dev, base):
        return [
            remote(block, block, g_sem.at[0, base + k], g_sem.at[1, base + k], dev(k)) for k in range(1, n)
        ]

    def finish(copies):
        for cp in copies:
            cp.wait()

    x_rows = pl.ds(pl.multiple_of(x * n_rows, 16), n_rows)
    x_copies = []

    def forward(n):
        k = order[n]
        finish(row_copies[k])
        if k:
            x_copies.append(
                remote(
                    rows.at[:, columns(k)], gathered.at[x_rows], x_sem.at[0, k - 1], x_sem.at[1, k - 1],
                    (at(xx=turn(x, k, nx)), e),
                )
            )
        val = dot(rows[:, columns(k)], weights[:, columns(k)], ((1,), (1,)))
        if n == 0:
            pre[...] = val
        else:
            pre[...] += val

    g_copies = share(g_all.at[y, x, c], nc, lambda k: (at(cc=turn(c, k, nc)), e), 0)
    finish(w_copies)
    reorder(raw, weights, 512)
    forward(0)
    finish(g_copies)
    g_copies = share(g_all.at[y, x], nx, lambda k: (at(xx=turn(x, k, nx)), e), 8)
    for n in range(1, nx - 2):
        forward(n)
    finish(g_copies)
    g_copies = share(g_all.at[y], ny, lambda k: (at(yy=turn(y, k, ny)), e), 16)

    finish(meta_copies)
    r_all = iota((n_rows, lanes), 0)
    in_main = r_all < n_main
    src_all = jnp.where(in_main, r_all // main, (r_all - n_main) // rest)
    slot_all = jnp.where(in_main, r_all % main, main + (r_all - n_main) % rest)
    same = one_hot(iota((lanes, lanes), 0) % 64 == iota((lanes, lanes), 1) % 64)
    g_src = [slot_of(meta_all[s]) for s in range(ne)]
    prob = jnp.zeros((n_rows, 1), F32)
    mine = []
    for s in range(ne):
        hit = (src_all == s) & (slot_all + e * slots == g_src[s])
        prob = prob + jnp.sum(jnp.where(hit, meta_all[s][1:2, :], 0.0), axis=1, keepdims=True)
        mine.append(dot(one_hot(hit), same).astype(BF16))
    links = []
    for q in range(ne):
        total = jnp.zeros((n_rows, n_rows), F32)
        for s in range(ne):
            hit = one_hot((src_all == s) & (slot_all + q * slots == g_src[s]))
            total = total + dot(mine[s], hit, ((1,), (1,)))
        links.append(total.astype(BF16))

    if nx > 2:
        forward(nx - 2)
    finish(g_copies)
    flat_g = g_all[...].reshape(plane * g_rows, 128).astype(BF16)
    p_row = iota((128, plane * g_rows), 0)
    p_col = iota((128, plane * g_rows), 1)
    for q in range(ne):
        perm = one_hot(p_col == (p_row // r2) * g_rows + q * r2 + p_row % r2)
        g_own[q] = dot(perm, flat_g).astype(BF16)
    forward(nx - 1)

    gate_pre, up_pre = pre[:, 0:128], pre[:, 128:256]
    gate_tan, up_tan = pre[:, 256:384], pre[:, 384:512]
    sigmoid = jax.nn.sigmoid(gate_pre)
    silu_val = gate_pre * sigmoid
    slope_up = sigmoid * (1.0 + gate_pre * (1.0 - sigmoid)) * up_pre
    hidden_tan = slope_up * gate_tan + silu_val * up_tan
    valid = (iota((n_rows, 128), 1) // 64) == jnp.where(slot_all >= cap, 1, 0)
    scaled_all[e] = jnp.where(valid, prob * hidden_tan, 0.0).astype(BF16)
    sc_copies = [
        remote(scaled_all.at[e], scaled_all.at[e], sc_sem.at[0, k - 1], sc_sem.at[1, k - 1], (dp, turn(e, k, ne)))
        for k in range(1, ne)
    ]
    for cp in sc_copies:
        cp.wait()
    pulled = jnp.zeros((n_rows, 128), F32)
    for q in range(ne):
        pulled = pulled + dot(dot(links[q], scaled_all[q]).astype(BF16), g_own[q])
    weighted = jnp.where(valid, prob * pulled, 0.0)
    coef_gate = weighted * slope_up
    coef_up = weighted * silu_val
    low = iota((n_rows, 128), 1) < 64
    first_expert = slot_all < cap
    coef_all[x] = jnp.where(
        low,
        jnp.where(first_expert, coef_gate, pltpu.roll(coef_gate, 64, 1)),
        jnp.where(first_expert, pltpu.roll(coef_up, 64, 1), coef_up),
    ).astype(BF16)
    coef_copies = [
        remote(coef_all.at[x], coef_all.at[x], coef_sem.at[0, k - 1], coef_sem.at[1, k - 1], (at(xx=turn(x, k, nx)), e))
        for k in range(1, nx)
    ]
    gathered[x_rows] = rows[:, columns(0)]
    for cp in x_copies + coef_copies:
        cp.wait()
    for i in range(nx):
        val = coef_all[i]
        coefs[i * n_rows : (i + 1) * n_rows, 0:128] = jnp.where(first_expert, val, jnp.zeros_like(val))
        coefs[i * n_rows : (i + 1) * n_rows, 128:256] = jnp.where(first_expert, jnp.zeros_like(val), val)

    span = cw // ny
    half_y = y // 2
    parity = y % 2
    pairs = [2, 1, 3, 0] if ny == 8 else list(range(1, ny // 2)) + [0]
    core_copies, y_copies = {}, {}

    def product(m):
        i = lax.rem(half_y + m, ny // 2)
        lhs = gathered[:, pl.ds(pl.multiple_of(i * 2 * span, 128), 2 * span)]
        part = dot(lhs, coefs[...], ((0,), (0,)))
        both = pl.ds(2 * i, 2)
        partial[both] = part.reshape(2, nz, nc, own, 256)
        if nc == 2:
            core_send[both] = partial[both, :, 1 - c].astype(BF16)
            core_copies[m] = remote(
                core_send.at[both], core_recv.at[both], core_sem.at[0, m], core_sem.at[1, m], (at(cc=1 - c), e)
            )

    def summed(t):
        val = partial[t, :, c]
        return val + core_recv[t].astype(F32) if nc == 2 else val

    def send_on(m):
        i = lax.rem(half_y + m, ny // 2)
        if nc == 2:
            core_copies[m].wait()
        for b in (1, 0):
            t = 2 * i + (parity + b) % 2
            j = 2 * m + b
            if j == 0:
                z_acc[...] = summed(t)
            else:
                ring_s[j - 1] = summed(t).astype(BF16)
                y_copies[j] = remote(
                    ring_s.at[j - 1], ring_r.at[j - 1], rs_sem.at[0, j - 1], rs_sem.at[1, j - 1], (at(yy=t), e)
                )

    for n, m in enumerate(pairs):
        product(m)
        if n:
            send_on(pairs[n - 1])
    send_on(pairs[-1])
    total = z_acc[...]
    for j, cp in y_copies.items():
        cp.wait()
        total = total + ring_r[j - 1].astype(F32)
    z_acc[...] = total

    result = z_acc[zh]
    z_copies = []
    for k in range(1, nz):
        t = turn(zh, k, nz)
        z_send[k - 1] = z_acc[t].astype(BF16)
        z_copies.append(
            remote(z_send.at[k - 1], z_recv.at[k - 1], z_sem.at[0, k - 1], z_sem.at[1, k - 1], (at(zz=t), e))
        )
    for k, cp in enumerate(z_copies):
        cp.wait()
        result = result + z_recv[k].astype(F32)
    out_ref[...] = result


def fused(cfg, ids, probs, tokens, mats):
    ny, nz, nx, nc, ne, cap = cfg
    width = tokens.shape[1]
    slots = 2 * cap
    main = slots // 16 * 16
    tail_parts = 16 // (slots - main)
    n_rows = ne * slots
    r2 = 128 // (ny * nx * nc)
    own = width // (ny * nz * nx * nc)
    part = (16, width * r2 // 16)
    vmem, dma = pltpu.VMEM, pltpu.SemaphoreType.DMA
    vspec = pl.BlockSpec(memory_space=pltpu.VMEM)
    hspec = pl.BlockSpec(memory_space=pl.ANY)
    hx, hy, hz = max(nx - 1, 1), max(ny - 1, 1), max(nz - 1, 1)
    return pl.pallas_call(
        functools.partial(kernel, cfg),
        out_shape=jax.ShapeDtypeStruct((own, 256), F32),
        in_specs=[vspec] * 3 + [hspec] * 5,
        out_specs=vspec,
        scratch_shapes=[
            vmem((8, 128), F32),
            vmem((ne, 8, 128), F32),
            vmem(part, BF16),
            vmem((ne,) + part, BF16),
            vmem((512, width), BF16),
            vmem((512, width), BF16),
            vmem((128, width), BF16),
            vmem(tokens.shape, BF16),
            vmem((ne, main, width), BF16),
            vmem((ne, 16, width // tail_parts), BF16),
            vmem((n_rows, width), BF16),
            vmem((ne, 16, width // tail_parts), BF16),
            vmem((n_rows, 512), F32),
            vmem((ny, nx, nc, ne * r2, 128), F32),
            vmem((ne, 128, 128), BF16),
            vmem((ne, n_rows, 128), BF16),
            vmem((nx * n_rows, width // nx), BF16),
            vmem((nx, n_rows, 128), BF16),
            vmem((nx * n_rows, 256), BF16),
            vmem((ny, nz, nc, own, 256), F32),
            vmem((ny, nz, own, 256), BF16),
            vmem((ny, nz, own, 256), BF16),
            vmem((nz, own, 256), F32),
            vmem((hz, own, 256), BF16),
            vmem((hz, own, 256), BF16),
            vmem((hy, nz, own, 256), BF16),
            vmem((hy, nz, own, 256), BF16),
            dma((5,)),
            dma((2, ne - 1)),
            dma((2, ne - 1)),
            dma((2, nx, ne - 1)),
            dma((2, ne - 1)),
            dma((2, hx)),
            dma((2, ne - 1)),
            dma((2, hx)),
            dma((2, ny)),
            dma((2, 24)),
            dma((2, hy)),
            dma((2, hz)),
        ],
        compiler_params=pltpu.CompilerParams(
            collective_id=0, has_side_effects=True, vmem_limit_bytes=58 * 2**20
        ),
    )(ids, probs, tokens, *mats)


def body(cfg, tokens, expert_ids, gate_probs, w_gate, w_up, w_down, v_gate, v_up):
    ny, nz, nx, nc, ne, cap = cfg
    width = tokens.shape[1]
    total_tokens = tokens.shape[0] * ny * nz * nx * nc * ne
    mats = [w.reshape(128, width) for w in (w_gate, w_up, v_gate, v_up, w_down)]
    return fused(cfg, expert_ids.T, gate_probs.T, tokens, mats) * (1.0 / total_tokens)


def solution(mesh, grid=GRID):
    cfg = grid + (mesh.shape["expert"], 18)
    return jax.shard_map(
        functools.partial(body, cfg),
        mesh=mesh,
        in_specs=(
            P(("dp", "expert"), None),
            P(("dp", "expert"), None),
            P(("dp", "expert"), None),
            P("expert", None, None),
            P("expert", None, None),
            P("expert", None, None),
            P("expert", None, None),
            P("expert", None, None),
        ),
        out_specs=P("dp", "expert"),
        check_vma=False,
    )
```

time: 108 us -> 96.8 us (0.90)
  the two profiles are of different devices: /device:TPU:2 before, /device:TPU:1 now
where the time goes in v2:
time: 96.8 us; the launch traced here: 96.3 us
  Pallas kernels  95 us (98%)
  other arithmetic  1.38 us (1%)
    pallas_call x1, Pallas kernels, fused(): pl.pallas_call(functools.partial(kernel, cfg), out_shape=jax.ShapeDtypeSt...  95 us

profile of v2, /device:TPU:1, one launch (start us, length us, event | category | flops | bytes accessed | tf_op | source)
XLA Modules:
  0.0 96.3 jit_solution(1859752906465257813)
XLA Ops:
  0.0 95.0 %shard_map.82 = f32[32,256]{1,0:T(8,128)} custom-call(s32[2,64]{1,0:T(2,128)} %bitcast.12, f32[2,64]{1,0:T(2,128)} %bitcast.13, bf16[64,6144]{1,0:T(8,128)(2,1)} %tokens_ref.1, bf16[128,6144]{1,0:T(8,128)(2,1)} %bitcast.7, bf16[128,6144]{1,0:T(8,128)(2,1)} %bitcast.8, bf16[128,6144]{1,0:T(8,128)(2,1)} %bitcast.9, bf16[128,6144]{1,0:T(8,128)(2,1)} %bitcast.10, ...), custom_call_target="tpu_custom_call" | custom-call | tf_op jit(solution)/shard_map/pallas_call | solution.py:420
  95.0 1.4 %broadcast_multiply_fusion = f32[32,256]{1,0:T(8,128)} fusion(f32[32,256]{1,0:T(8,128)} %shard_map.82), kind=kLoop, calls=%fused_computation | loop fusion | flops 8192 | bytes 65536 | tf_op jit(solution)/shard_map/mul | solution.py:477

commit v3 on v2

--- a/solution.py
+++ b/solution.py
@@ -29,7 +29,7 @@
     ids_ref, probs_ref, tokens_ref, wg_ref, wu_ref, vg_ref, vu_ref, wd_ref,
     out_ref,
     meta_own, meta_all, part_own, parts, raw, weights, down, ordered, sent, sent_tail, rows, tails, pre,
-    g_all, g_own, scaled_all, gathered, coef_all, coefs, partial, core_send, core_recv,
+    g_all, g_own, links, scaled_all, gathered, coef_all, coefs, partial, core_send, core_recv,
     z_acc, z_send, z_recv, ring_s, ring_r,
     w_sem, meta_sem, part_sem, row_sem, tail_sem, x_sem, sc_sem, coef_sem, core_sem, g_sem, rs_sem, z_sem,
 ):
@@ -178,19 +178,6 @@
             remote(meta_own, meta_all.at[e], meta_sem.at[0, j - 1], meta_sem.at[1, j - 1], (dp, turn(e, j, ne)))
         )
     row_copies[order[0]] = send_rows(order[0])
-    tail_val = jnp.zeros((n_tail, tw), F32)
-    for q in range(tail_parts):
-        pick = dot(one_hot(hit_tail & (q_tail == q)), half).astype(BF16)
-        tail_val = tail_val + dot(pick, ordered[:, q * tw : (q + 1) * tw])
-    tail_val = tail_val.astype(BF16)
-    for d in range(ne):
-        sent_tail[d] = tail_val[d * 16 : (d + 1) * 16]
-    for j in z_order:
-        d = turn(e, j, ne)
-        tail_copies.append(
-            remote(sent_tail.at[d], tails.at[e], tail_sem.at[0, j - 1], tail_sem.at[1, j - 1], (dp, d))
-        )
-    tails[e] = sent_tail[e]
     down_copy.wait()
     s_row = iota((16, 128), 0)
     s_col = iota((16, 128), 1)
@@ -205,6 +192,19 @@
         part_copies.append(
             remote(part_own, parts.at[e], part_sem.at[0, j - 1], part_sem.at[1, j - 1], (dp, turn(e, j, ne)))
         )
+    tail_val = jnp.zeros((n_tail, tw), F32)
+    for q in range(tail_parts):
+        pick = dot(one_hot(hit_tail & (q_tail == q)), half).astype(BF16)
+        tail_val = tail_val + dot(pick, ordered[:, q * tw : (q + 1) * tw])
+    tail_val = tail_val.astype(BF16)
+    for d in range(ne):
+        sent_tail[d] = tail_val[d * 16 : (d + 1) * 16]
+    for j in z_order:
+        d = turn(e, j, ne)
+        tail_copies.append(
+            remote(sent_tail.at[d], tails.at[e], tail_sem.at[0, j - 1], tail_sem.at[1, j - 1], (dp, d))
+        )
+    tails[e] = sent_tail[e]
     for k in order[1:]:
         place_rows(k)
         row_copies[k] = send_rows(k)
@@ -217,6 +217,39 @@
     for q in range(tail_parts):
         hit = (t_row // rest == t_col // 16) & (t_col % 16 == q * rest + t_row % rest)
         rows[n_main:n_rows, q * tw : (q + 1) * tw] = dot(one_hot(hit), flat_tails).astype(BF16)
+
+    def share(block, n, dev, base):
+        return [
+            remote(block, block, g_sem.at[0, base + k], g_sem.at[1, base + k], dev(k)) for k in range(1, n)
+        ]
+
+    def finish(copies):
+        for cp in copies:
+            cp.wait()
+
+    x_rows = pl.ds(pl.multiple_of(x * n_rows, 16), n_rows)
+    x_copies = []
+
+    def forward(n):
+        k = order[n]
+        finish(row_copies[k])
+        if k:
+            x_copies.append(
+                remote(
+                    rows.at[:, columns(k)], gathered.at[x_rows], x_sem.at[0, k - 1], x_sem.at[1, k - 1],
+                    (at(xx=turn(x, k, nx)), e),
+                )
+            )
+
+    def multiply(n):
+        k = order[n]
+        val = dot(rows[:, columns(k)], weights[:, columns(k)], ((1,), (1,)))
+        if n == 0:
+            pre[...] = val
+        else:
+            pre[...] += val
+
+    forward(0)
 
     for cp in part_copies:
         cp.wait()
@@ -231,44 +264,19 @@
     collect = jnp.where((from_row // 16 == to_row // r2) & (from_row % r2 == to_row % r2), 1.0, 0.0)
     g_all[y, x, c] = dot(collect, acc, precision=lax.Precision.HIGHEST)
 
-    def share(block, n, dev, base):
-        return [
-            remote(block, block, g_sem.at[0, base + k], g_sem.at[1, base + k], dev(k)) for k in range(1, n)
-        ]
-
-    def finish(copies):
-        for cp in copies:
-            cp.wait()
-
-    x_rows = pl.ds(pl.multiple_of(x * n_rows, 16), n_rows)
-    x_copies = []
-
-    def forward(n):
-        k = order[n]
-        finish(row_copies[k])
-        if k:
-            x_copies.append(
-                remote(
-                    rows.at[:, columns(k)], gathered.at[x_rows], x_sem.at[0, k - 1], x_sem.at[1, k - 1],
-                    (at(xx=turn(x, k, nx)), e),
-                )
-            )
-        val = dot(rows[:, columns(k)], weights[:, columns(k)], ((1,), (1,)))
-        if n == 0:
-            pre[...] = val
-        else:
-            pre[...] += val
-
     g_copies = share(g_all.at[y, x, c], nc, lambda k: (at(cc=turn(c, k, nc)), e), 0)
     finish(w_copies)
     reorder(raw, weights, 512)
-    forward(0)
+    multiply(0)
     finish(g_copies)
     g_copies = share(g_all.at[y, x], nx, lambda k: (at(xx=turn(x, k, nx)), e), 8)
     for n in range(1, nx - 2):
         forward(n)
     finish(g_copies)
     g_copies = share(g_all.at[y], ny, lambda k: (at(yy=turn(y, k, ny)), e), 16)
+
+    for n in range(1, nx - 2):
+        multiply(n)
 
     finish(meta_copies)
     r_all = iota((n_rows, lanes), 0)
@@ -283,16 +291,36 @@
         hit = (src_all == s) & (slot_all + e * slots == g_src[s])
         prob = prob + jnp.sum(jnp.where(hit, meta_all[s][1:2, :], 0.0), axis=1, keepdims=True)
         mine.append(dot(one_hot(hit), same).astype(BF16))
-    links = []
     for q in range(ne):
         total = jnp.zeros((n_rows, n_rows), F32)
         for s in range(ne):
             hit = one_hot((src_all == s) & (slot_all + q * slots == g_src[s]))
             total = total + dot(mine[s], hit, ((1,), (1,)))
-        links.append(total.astype(BF16))
+        links[q] = total.astype(BF16)
 
     if nx > 2:
         forward(nx - 2)
+        multiply(nx - 2)
+    forward(nx - 1)
+    multiply(nx - 1)
+
+    gate_pre, up_pre = pre[:, 0:128], pre[:, 128:256]
+    gate_tan, up_tan = pre[:, 256:384], pre[:, 384:512]
+    sigmoid = jax.nn.sigmoid(gate_pre)
+    silu_val = gate_pre * sigmoid
+    slope_up = sigmoid * (1.0 + gate_pre * (1.0 - sigmoid)) * up_pre
+    hidden_tan = slope_up * gate_tan + silu_val * up_tan
+    valid = (iota((n_rows, 128), 1) // 64) == jnp.where(slot_all >= cap, 1, 0)
+    low = iota((n_rows, 128), 1) < 64
+    fold = n_rows // 2 + (-n_rows // 2) % 16
+    scaled = jnp.where(valid, prob * hidden_tan, 0.0)
+    both_halves = scaled + pltpu.roll(scaled, 64, 1)
+    upper_rows = jnp.concatenate([both_halves[fold:], jnp.zeros((2 * fold - n_rows, 128), F32)], axis=0)
+    scaled_all[e] = jnp.where(low[:fold], both_halves[:fold], upper_rows).astype(BF16)
+    sc_copies = [
+        remote(scaled_all.at[e], scaled_all.at[e], sc_sem.at[0, k - 1], sc_sem.at[1, k - 1], (dp, turn(e, k, ne)))
+        for k in range(1, ne)
+    ]
     finish(g_copies)
     flat_g = g_all[...].reshape(plane * g_rows, 128).astype(BF16)
     p_row = iota((128, plane * g_rows), 0)
@@ -300,46 +328,44 @@
     for q in range(ne):
         perm = one_hot(p_col == (p_row // r2) * g_rows + q * r2 + p_row % r2)
         g_own[q] = dot(perm, flat_g).astype(BF16)
-    forward(nx - 1)
-
-    gate_pre, up_pre = pre[:, 0:128], pre[:, 128:256]
-    gate_tan, up_tan = pre[:, 256:384], pre[:, 384:512]
-    sigmoid = jax.nn.sigmoid(gate_pre)
-    silu_val = gate_pre * sigmoid
-    slope_up = sigmoid * (1.0 + gate_pre * (1.0 - sigmoid)) * up_pre
-    hidden_tan = slope_up * gate_tan + silu_val * up_tan
-    valid = (iota((n_rows, 128), 1) // 64) == jnp.where(slot_all >= cap, 1, 0)
-    scaled_all[e] = jnp.where(valid, prob * hidden_tan, 0.0).astype(BF16)
-    sc_copies = [
-        remote(scaled_all.at[e], scaled_all.at[e], sc_sem.at[0, k - 1], sc_sem.at[1, k - 1], (dp, turn(e, k, ne)))
-        for k in range(1, ne)
-    ]
-    for cp in sc_copies:
-        cp.wait()
-    pulled = jnp.zeros((n_rows, 128), F32)
-    for q in range(ne):
-        pulled = pulled + dot(dot(links[q], scaled_all[q]).astype(BF16), g_own[q])
+    pulled = dot(dot(links[e], scaled.astype(BF16)).astype(BF16), g_own[e])
+    gathered[x_rows] = rows[:, columns(0)]
+    for k in range(1, ne):
+        sc_copies[k - 1].wait()
+        q = turn(e, -k, ne)
+        packed = scaled_all[q].astype(F32)
+        turned = pltpu.roll(packed, 64, 1)
+        spread = jnp.concatenate(
+            [jnp.where(low[:fold], packed, turned), jnp.where(low[:fold], turned, packed)[: n_rows - fold]], axis=0
+        )
+        spread = jnp.where(valid, spread, 0.0).astype(BF16)
+        pulled = pulled + dot(dot(links[q], spread).astype(BF16), g_own[q])
     weighted = jnp.where(valid, prob * pulled, 0.0)
     coef_gate = weighted * slope_up
     coef_up = weighted * silu_val
-    low = iota((n_rows, 128), 1) < 64
     first_expert = slot_all < cap
-    coef_all[x] = jnp.where(
+    coef_mine = jnp.where(
         low,
         jnp.where(first_expert, coef_gate, pltpu.roll(coef_gate, 64, 1)),
         jnp.where(first_expert, pltpu.roll(coef_up, 64, 1), coef_up),
     ).astype(BF16)
+    coef_all[x] = coef_mine
     coef_copies = [
         remote(coef_all.at[x], coef_all.at[x], coef_sem.at[0, k - 1], coef_sem.at[1, k - 1], (at(xx=turn(x, k, nx)), e))
         for k in range(1, nx)
     ]
-    gathered[x_rows] = rows[:, columns(0)]
-    for cp in x_copies + coef_copies:
-        cp.wait()
-    for i in range(nx):
-        val = coef_all[i]
-        coefs[i * n_rows : (i + 1) * n_rows, 0:128] = jnp.where(first_expert, val, jnp.zeros_like(val))
-        coefs[i * n_rows : (i + 1) * n_rows, 128:256] = jnp.where(first_expert, jnp.zeros_like(val), val)
+
+    def place_coefs(i, val):
+        here = pl.ds(pl.multiple_of(i * n_rows, 16), n_rows)
+        coefs[here, 0:128] = jnp.where(first_expert, val, jnp.zeros_like(val))
+        coefs[here, 128:256] = jnp.where(first_expert, jnp.zeros_like(val), val)
+
+    place_coefs(x, coef_mine)
+    finish(x_copies)
+    for k in range(1, nx):
+        coef_copies[k - 1].wait()
+        i = turn(x, -k, nx)
+        place_coefs(i, coef_all[i])
 
     span = cw // ny
     half_y = y // 2
@@ -438,7 +464,8 @@
             vmem((n_rows, 512), F32),
             vmem((ny, nx, nc, ne * r2, 128), F32),
             vmem((ne, 128, 128), BF16),
-            vmem((ne, n_rows, 128), BF16),
+            vmem((ne, n_rows, n_rows), BF16),
+            vmem((ne, (n_rows // 2 + 15) // 16 * 16, 128), BF16),
             vmem((nx * n_rows, width // nx), BF16),
             vmem((nx, n_rows, 128), BF16),
             vmem((nx * n_rows, 256), BF16),

time: 96.8 us -> 90.1 us (0.931)
  Pallas kernels: 95 us -> 88.5 us
    pallas_call x1, Pallas kernels: 95 us -> 88.5 us  [fused(): pl.pallas_call(functools.partial(kernel, cfg), out_shape=jax.ShapeDtypeSt...]
where the time goes in v3:
time: 90.1 us; the launch traced here: 89.9 us
  Pallas kernels  88.5 us (98%)
  other arithmetic  1.38 us (2%)
    pallas_call x1, Pallas kernels, fused(): pl.pallas_call(functools.partial(kernel, cfg), out_shape=jax.ShapeDtypeSt...  88.5 us

profile of v3, /device:TPU:1, one launch (start us, length us, event | category | flops | bytes accessed | tf_op | source)
XLA Modules:
  0.0 89.9 jit_solution(10418037132798452013)
XLA Ops:
  0.0 88.5 %shard_map.82 = f32[32,256]{1,0:T(8,128)} custom-call(s32[2,64]{1,0:T(2,128)} %bitcast.12, f32[2,64]{1,0:T(2,128)} %bitcast.13, bf16[64,6144]{1,0:T(8,128)(2,1)} %tokens_ref.1, bf16[128,6144]{1,0:T(8,128)(2,1)} %bitcast.7, bf16[128,6144]{1,0:T(8,128)(2,1)} %bitcast.8, bf16[128,6144]{1,0:T(8,128)(2,1)} %bitcast.9, bf16[128,6144]{1,0:T(8,128)(2,1)} %bitcast.10, ...), custom_call_target="tpu_custom_call" | custom-call | tf_op jit(solution)/shard_map/pallas_call | solution.py:446
  88.5 1.4 %broadcast_multiply_fusion = f32[32,256]{1,0:T(8,128)} fusion(f32[32,256]{1,0:T(8,128)} %shard_map.82), kind=kLoop, calls=%fused_computation | loop fusion | flops 8192 | bytes 65536 | tf_op jit(solution)/shard_map/mul | solution.py:504

commit v4 on v3

--- a/solution.py
+++ b/solution.py
@@ -26,9 +26,9 @@
 
 def kernel(
     cfg,
-    ids_ref, probs_ref, tokens_ref, wg_ref, wu_ref, vg_ref, vu_ref, wd_ref,
+    ids_ref, probs_ref, tokens_hbm, wg_ref, wu_ref, vg_ref, vu_ref, wd_ref,
     out_ref,
-    meta_own, meta_all, part_own, parts, raw, weights, down, ordered, sent, sent_tail, rows, tails, pre,
+    tokens_ref, meta_own, meta_all, part_own, parts, raw, weights, down, ordered, sent, sent_tail, rows, tails, pre,
     g_all, g_own, links, scaled_all, gathered, coef_all, coefs, partial, core_send, core_recv,
     z_acc, z_send, z_recv, ring_s, ring_r,
     w_sem, meta_sem, part_sem, row_sem, tail_sem, x_sem, sc_sem, coef_sem, core_sem, g_sem, rs_sem, z_sem,
@@ -71,14 +71,15 @@
         copy.start()
         return copy
 
-    w_copies = []
-    for m, ref in enumerate((wg_ref, wu_ref, vg_ref, vu_ref)):
-        cp = pltpu.make_async_copy(ref, raw.at[pl.ds(m * 128, 128)], w_sem.at[m])
-        cp.start()
-        w_copies.append(cp)
-    down_copy = pltpu.make_async_copy(wd_ref, down, w_sem.at[4])
-    down_copy.start()
-
+    pending = []
+
+    def arrived(copies):
+        for cp in copies:
+            cp.wait_recv()
+            pending.append(cp)
+
+    token_copy = pltpu.make_async_copy(tokens_hbm, tokens_ref, w_sem.at[5])
+    token_copy.start()
     peers = [(dp, turn(e, k, ne)) for k in range(1, ne)]
     for k in range(1, ny):
         peers.append((at(yy=turn(y, k, ny)), e))
@@ -91,6 +92,14 @@
     barrier = pltpu.get_barrier_semaphore()
     for dev in peers:
         pl.semaphore_signal(barrier, inc=1, device_id=dev, device_id_type=pl.DeviceIdType.MESH)
+    w_copies = []
+    for m, ref in enumerate((wg_ref, wu_ref, vg_ref, vu_ref)):
+        cp = pltpu.make_async_copy(ref, raw.at[pl.ds(m * 128, 128)], w_sem.at[m])
+        cp.start()
+        w_copies.append(cp)
+    down_copy = pltpu.make_async_copy(wd_ref, down, w_sem.at[4])
+    down_copy.start()
+
 
     lanes = 128
     upper = one_hot(iota((lanes, lanes), 0) < iota((lanes, lanes), 1))
@@ -141,6 +150,7 @@
 
         lax.fori_loop(0, ny * nz // 2, pair, 0)
 
+    token_copy.wait()
     reorder(tokens_ref, ordered, tokens_ref.shape[0])
 
     order = [2, 1, 3, 0] if nx == 4 else list(range(1, nx)) + [0]
@@ -148,6 +158,12 @@
 
     def columns(k):
         return pl.ds(pl.multiple_of(turn(x, k, nx) * cw, 128), cw)
+
+    def pieces(k):
+        if k or cw % 256:
+            return [(k, columns(k))]
+        start = x * cw
+        return [(s, pl.ds(pl.multiple_of(start + h * (cw // 2), 128), cw // 2)) for h, s in ((0, 0), (1, nx))]
 
     def place_rows(k):
         val = dot(pick_main, ordered[:, columns(k)]).astype(BF16)
@@ -157,17 +173,15 @@
     my_rows = pl.ds(pl.multiple_of(e * main, 16), main)
 
     def send_rows(k):
-        got = []
-        for j in z_order:
-            d = turn(e, j, ne)
-            got.append(
-                remote(
-                    sent.at[d, :, columns(k)], rows.at[my_rows, columns(k)],
-                    row_sem.at[0, k, j - 1], row_sem.at[1, k, j - 1], (dp, d),
-                )
+        rows[my_rows, columns(k)] = sent[e, :, columns(k)]
+        return [
+            remote(
+                sent.at[turn(e, j, ne), :, part], rows.at[my_rows, part],
+                row_sem.at[0, s, j - 1], row_sem.at[1, s, j - 1], (dp, turn(e, j, ne)),
             )
-        rows[my_rows, columns(k)] = sent[e, :, columns(k)]
-        return got
+            for s, part in pieces(k)
+            for j in z_order
+        ]
 
     place_rows(order[0])
     pl.semaphore_wait(barrier, len(peers))
@@ -209,8 +223,7 @@
         place_rows(k)
         row_copies[k] = send_rows(k)
 
-    for cp in tail_copies:
-        cp.wait()
+    arrived(tail_copies)
     t_row = iota((ne * rest, n_tail), 0)
     t_col = iota((ne * rest, n_tail), 1)
     flat_tails = tails[...].reshape(n_tail, tw)
@@ -223,16 +236,12 @@
             remote(block, block, g_sem.at[0, base + k], g_sem.at[1, base + k], dev(k)) for k in range(1, n)
         ]
 
-    def finish(copies):
-        for cp in copies:
-            cp.wait()
-
     x_rows = pl.ds(pl.multiple_of(x * n_rows, 16), n_rows)
     x_copies = []
 
     def forward(n):
         k = order[n]
-        finish(row_copies[k])
+        arrived(row_copies[k])
         if k:
             x_copies.append(
                 remote(
@@ -243,16 +252,16 @@
 
     def multiply(n):
         k = order[n]
-        val = dot(rows[:, columns(k)], weights[:, columns(k)], ((1,), (1,)))
-        if n == 0:
-            pre[...] = val
-        else:
-            pre[...] += val
+        for _, part in pieces(k):
+            val = dot(rows[:, part], weights[:, part], ((1,), (1,)))
+            if n == 0:
+                pre[...] = val
+            else:
+                pre[...] += val
 
     forward(0)
 
-    for cp in part_copies:
-        cp.wait()
+    arrived(part_copies)
     gw = parts[...].reshape(ne * 16, pw)
     acc = jnp.zeros((ne * 16, 128), F32)
     r_part = iota((ne * 16, 128), 0) % 16 // r2
@@ -265,20 +274,21 @@
     g_all[y, x, c] = dot(collect, acc, precision=lax.Precision.HIGHEST)
 
     g_copies = share(g_all.at[y, x, c], nc, lambda k: (at(cc=turn(c, k, nc)), e), 0)
-    finish(w_copies)
+    for cp in w_copies:
+        cp.wait()
     reorder(raw, weights, 512)
     multiply(0)
-    finish(g_copies)
+    arrived(g_copies)
     g_copies = share(g_all.at[y, x], nx, lambda k: (at(xx=turn(x, k, nx)), e), 8)
     for n in range(1, nx - 2):
         forward(n)
-    finish(g_copies)
+    arrived(g_copies)
     g_copies = share(g_all.at[y], ny, lambda k: (at(yy=turn(y, k, ny)), e), 16)
 
     for n in range(1, nx - 2):
         multiply(n)
 
-    finish(meta_copies)
+    arrived(meta_copies)
     r_all = iota((n_rows, lanes), 0)
     in_main = r_all < n_main
     src_all = jnp.where(in_main, r_all // main, (r_all - n_main) // rest)
@@ -301,8 +311,9 @@
     if nx > 2:
         forward(nx - 2)
         multiply(nx - 2)
-    forward(nx - 1)
-    multiply(nx - 1)
+    for h, (_, part) in enumerate(pieces(0)):
+        arrived(row_copies[0][h * (ne - 1) : (h + 1) * (ne - 1)])
+        pre[...] += dot(rows[:, part], weights[:, part], ((1,), (1,)))
 
     gate_pre, up_pre = pre[:, 0:128], pre[:, 128:256]
     gate_tan, up_tan = pre[:, 256:384], pre[:, 384:512]
@@ -321,7 +332,7 @@
         remote(scaled_all.at[e], scaled_all.at[e], sc_sem.at[0, k - 1], sc_sem.at[1, k - 1], (dp, turn(e, k, ne)))
         for k in range(1, ne)
     ]
-    finish(g_copies)
+    arrived(g_copies)
     flat_g = g_all[...].reshape(plane * g_rows, 128).astype(BF16)
     p_row = iota((128, plane * g_rows), 0)
     p_col = iota((128, plane * g_rows), 1)
@@ -331,7 +342,7 @@
     pulled = dot(dot(links[e], scaled.astype(BF16)).astype(BF16), g_own[e])
     gathered[x_rows] = rows[:, columns(0)]
     for k in range(1, ne):
-        sc_copies[k - 1].wait()
+        arrived(sc_copies[k - 1 : k])
         q = turn(e, -k, ne)
         packed = scaled_all[q].astype(F32)
         turned = pltpu.roll(packed, 64, 1)
@@ -361,9 +372,9 @@
         coefs[here, 128:256] = jnp.where(first_expert, jnp.zeros_like(val), val)
 
     place_coefs(x, coef_mine)
-    finish(x_copies)
+    arrived(x_copies)
     for k in range(1, nx):
-        coef_copies[k - 1].wait()
+        arrived(coef_copies[k - 1 : k])
         i = turn(x, -k, nx)
         place_coefs(i, coef_all[i])
 
@@ -392,7 +403,7 @@
     def send_on(m):
         i = lax.rem(half_y + m, ny // 2)
         if nc == 2:
-            core_copies[m].wait()
+            arrived([core_copies[m]])
         for b in (1, 0):
             t = 2 * i + (parity + b) % 2
             j = 2 * m + b
@@ -411,7 +422,7 @@
     send_on(pairs[-1])
     total = z_acc[...]
     for j, cp in y_copies.items():
-        cp.wait()
+        arrived([cp])
         total = total + ring_r[j - 1].astype(F32)
     z_acc[...] = total
 
@@ -424,9 +435,11 @@
             remote(z_send.at[k - 1], z_recv.at[k - 1], z_sem.at[0, k - 1], z_sem.at[1, k - 1], (at(zz=t), e))
         )
     for k, cp in enumerate(z_copies):
-        cp.wait()
+        arrived([cp])
         result = result + z_recv[k].astype(F32)
     out_ref[...] = result
+    for cp in pending:
+        cp.wait_send()
 
 
 def fused(cfg, ids, probs, tokens, mats):
@@ -446,9 +459,10 @@
     return pl.pallas_call(
         functools.partial(kernel, cfg),
         out_shape=jax.ShapeDtypeStruct((own, 256), F32),
-        in_specs=[vspec] * 3 + [hspec] * 5,
+        in_specs=[vspec] * 2 + [hspec] * 6,
         out_specs=vspec,
         scratch_shapes=[
+            vmem(tokens.shape, BF16),
             vmem((8, 128), F32),
             vmem((ne, 8, 128), F32),
             vmem(part, BF16),
@@ -477,10 +491,10 @@
             vmem((hz, own, 256), BF16),
             vmem((hy, nz, own, 256), BF16),
             vmem((hy, nz, own, 256), BF16),
-            dma((5,)),
+            dma((6,)),
             dma((2, ne - 1)),
             dma((2, ne - 1)),
-            dma((2, nx, ne - 1)),
+            dma((2, nx + 1, ne - 1)),
             dma((2, ne - 1)),
             dma((2, hx)),
             dma((2, ne - 1)),

time: 90.1 us -> 89.8 us (level)
  no operation moved by 1% of the time
where the time goes in v4:
time: 89.8 us; the launch traced here: 89.6 us
  Pallas kernels  88.2 us (98%)
  other arithmetic  1.38 us (2%)
    pallas_call x1, Pallas kernels, fused(): pl.pallas_call(functools.partial(kernel, cfg), out_shape=jax.ShapeDtypeSt...  88.2 us

profile of v4, /device:TPU:1, one launch (start us, length us, event | category | flops | bytes accessed | tf_op | source)
XLA Modules:
  0.0 89.6 jit_solution(17850301916815563781)
XLA Ops:
  0.0 88.2 %shard_map.82 = f32[32,256]{1,0:T(8,128)} custom-call(s32[2,64]{1,0:T(2,128)} %bitcast.12, f32[2,64]{1,0:T(2,128)} %bitcast.13, bf16[64,6144]{1,0:T(8,128)(2,1)} %tokens_hbm.1, bf16[128,6144]{1,0:T(8,128)(2,1)} %bitcast.7, bf16[128,6144]{1,0:T(8,128)(2,1)} %bitcast.8, bf16[128,6144]{1,0:T(8,128)(2,1)} %bitcast.9, bf16[128,6144]{1,0:T(8,128)(2,1)} %bitcast.10, ...), custom_call_target="tpu_custom_call" | custom-call | tf_op jit(solution)/shard_map/pallas_call | solution.py:459
  88.2 1.4 %broadcast_multiply_fusion = f32[32,256]{1,0:T(8,128)} fusion(f32[32,256]{1,0:T(8,128)} %shard_map.82), kind=kLoop, calls=%fused_computation | loop fusion | flops 8192 | bytes 65536 | tf_op jit(solution)/shard_map/mul | solution.py:518
